TPU v7x, 32 devices: a whole 2x2x4 slice. The times are simulated.
32 devices in a mesh: rep: 4 (over z), exp: 8 (over y, x, core).
Axes of the slice: x: 2, y: 2, z: 4, core: 2. Of those that a mesh axis runs over, the one named last changes fastest.
Arguments:
- activations: bfloat16 [4096, 4096], P(('rep', 'exp')), may hold values from -6 to 6
- grad_hidden: bfloat16 [4096, 1024], P(('rep', 'exp')), may hold values from -6 to 6
- pre_gate: bfloat16 [4096, 1024], P(('rep', 'exp')), may hold values from -12 to 12
- pre_up: bfloat16 [4096, 1024], P(('rep', 'exp')), may hold values from -6 to 6
- modality: int32 [4096], P(('rep', 'exp')), may hold values from 0 to 1, as said below
- expert_index: int32 [4096], P(('rep', 'exp')), may hold values from 0 to 1
- master: float32 [16384, 2048], P(('exp', 'rep')), may hold values from -0.09375 to 0.09375
- first_moment: float32 [16384, 2048], P(('exp', 'rep')), may hold values from -18 to 18
- second_moment: float32 [16384, 2048], P(('exp', 'rep')), may hold values from 200 to 2000
Outputs:
- input_grad: bfloat16 [4096, 4096], P(('rep', 'exp'))
- new_master: float32 [16384, 2048], P(('exp', 'rep'))
- new_first: float32 [16384, 2048], P(('exp', 'rep'))
- new_second: float32 [16384, 2048], P(('exp', 'rep'))
Inputs may be any that keep to these rules, and one draw needn't show every extreme that they name: Among the 128 tokens of one device no expert 2 * modality + expert_index is named more than 48 times; in every replica group of 1024 tokens one expert is named exactly 48 times on every device.
All inputs are finite; a program needn't handle non-finite values.
Results may differ from a plain program's by a relative error of at most 0.019.
Values may be sent and summed in bfloat16 or wider, within the bound.
A program may use at most 128 MiB of HBM per device.

v0:
```python
import jax
import jax.numpy as jnp
from jax import lax
from jax.sharding import PartitionSpec as P

EXPERTS = 4
CAP = 48


beta_one = 0.9
beta_two = 0.999
learn_rate = 0.02
adam_eps = 1e-08
adam_count = 1000


def from_partner(block, axis, stride):
    count = lax.axis_size(axis)
    route = []
    for low in range(count):
        high = low | 1 << stride
        if high != low and high < count:
            route += [(low, high), (high, low)]
    return lax.ppermute(block, axis, route)


def hidden_grads(saved_rows):
    grad_val = saved_rows[:, 0].astype(jnp.float32)
    gate_val = saved_rows[:, 1].astype(jnp.float32)
    up_val = saved_rows[:, 2].astype(jnp.float32)
    sig = 1.0 / (1.0 + jnp.exp(-gate_val))
    grad_gate = (grad_val * up_val * sig * (1.0 + gate_val * (1.0 - sig))).astype(jnp.bfloat16)
    grad_up = (grad_val * gate_val * sig).astype(jnp.bfloat16)
    return jnp.stack([grad_gate, grad_up], axis=1)


def body(
    activations,
    grad_hidden,
    pre_gate,
    pre_up,
    modality,
    expert_index,
    master,
    first_moment,
    second_moment,
):
    tok_count = activations.shape[0]
    width = activations.shape[1]
    hidden = grad_hidden.shape[1]
    exp_size = lax.axis_size("exp")
    group = exp_size // EXPERTS
    piece_width = width // group
    piece_hidden = hidden // group
    capacity = CAP
    rows_total = exp_size * capacity
    expert = 2 * modality + expert_index
    onehot = (expert[:, None] == jnp.arange(EXPERTS, dtype=jnp.int32)[None, :]).astype(jnp.int32)
    before = jnp.cumsum(onehot, axis=0) - onehot
    slot_pos = jnp.sum(before * onehot, axis=1)
    same_expert = expert[None, None, :] == jnp.arange(EXPERTS, dtype=jnp.int32)[:, None, None]
    same_slot = slot_pos[None, None, :] == jnp.arange(capacity, dtype=jnp.int32)[None, :, None]
    routing = (same_expert & same_slot).astype(jnp.bfloat16)
    x_split = activations.reshape(tok_count, group, piece_width)
    x_send = jnp.einsum("ect,tgd->egcd", routing, x_split, preferred_element_type=jnp.float32)
    x_send = x_send.astype(jnp.bfloat16).reshape(EXPERTS * group, capacity, piece_width)
    saved = jnp.stack([grad_hidden, pre_gate, pre_up], axis=1)
    split_saved = saved.reshape(tok_count, 3, group, piece_hidden)
    parts = jnp.einsum("ect,tsgh->egcsh", routing, split_saved, preferred_element_type=jnp.float32)
    parts = parts.astype(jnp.bfloat16).reshape(EXPERTS * group, capacity, 3 * piece_hidden)
    x_recv, h_recv = (
        lax.all_to_all(x_send, "exp", split_axis=0, concat_axis=0, tiled=True),
        lax.all_to_all(parts, "exp", split_axis=0, concat_axis=0, tiled=True),
    )
    local = hidden_grads(h_recv.reshape(rows_total, 3, piece_hidden))
    blocks = local[None]
    position = lax.axis_index("exp")
    for level in range(group.bit_length() - 1):
        partner = from_partner(blocks, "exp", level)
        upper = position // 2**level % 2 == 1
        blocks = jnp.where(
            upper,
            jnp.concatenate([partner, blocks], axis=0),
            jnp.concatenate([blocks, partner], axis=0),
        )
    grads_flat = jnp.transpose(blocks, (1, 2, 0, 3)).reshape(rows_total, 2 * hidden)
    x_rows = x_recv.reshape(rows_total, piece_width)
    shard_bf = master.astype(jnp.bfloat16)
    dx_rows = lax.dot_general(
        grads_flat,
        lax.all_gather(shard_bf, "rep", axis=0, tiled=True),
        (((1,), (1,)), ((), ())),
        preferred_element_type=jnp.float32,
    )
    dx_send = dx_rows.astype(jnp.bfloat16).reshape(exp_size, capacity, piece_width)
    back = lax.all_to_all(dx_send, "exp", split_axis=0, concat_axis=0, tiled=True)
    back = back.reshape(EXPERTS, group, capacity, piece_width)
    input_grad = jnp.einsum("ect,egcd->tgd", routing, back, preferred_element_type=jnp.float32)
    input_grad = input_grad.reshape(tok_count, width).astype(jnp.bfloat16)
    weight_grad = lax.psum_scatter(
        lax.dot_general(
            x_rows, grads_flat, (((0,), (0,)), ((), ())), preferred_element_type=jnp.float32
        ).astype(jnp.bfloat16),
        "rep",
        scatter_dimension=0,
        tiled=True,
    ).astype(jnp.float32)
    new_first = beta_one * first_moment + (1.0 - beta_one) * weight_grad
    new_second = beta_two * second_moment + (1.0 - beta_two) * weight_grad * weight_grad
    corr_one = 1.0 - beta_one**adam_count
    corr_two = 1.0 - beta_two**adam_count
    update = new_first / corr_one / (jnp.sqrt(new_second / corr_two) + adam_eps)
    new_master = master - learn_rate * update
    return (input_grad, new_master, new_first, new_second)


def solution(mesh):
    in_specs = (
        P(("rep", "exp"), None),
        P(("rep", "exp"), None),
        P(("rep", "exp"), None),
        P(("rep", "exp"), None),
        P(("rep", "exp")),
        P(("rep", "exp")),
        P(("exp", "rep"), None),
        P(("exp", "rep"), None),
        P(("exp", "rep"), None),
    )
    out_specs = (
        P(("rep", "exp"), None),
        P(("exp", "rep"), None),
        P(("exp", "rep"), None),
        P(("exp", "rep"), None),
    )
    return jax.shard_map(body, mesh=mesh, in_specs=in_specs, out_specs=out_specs, check_vma=False)
```

profile of v0, /device:TPU:0, one launch (start us, length us, event | category | flops | bytes accessed | tf_op | source)
XLA Modules:
  0.0 420.5 jit_solution(10117294487956138449)
XLA Ops:
  7.2 0.0 copy-start.1
  7.2 0.7 multiply_add_fusion
  7.9 0.1 fusion.20
  8.0 0.2 reduce_window_sum.11
  8.2 0.2 select_reduce_fusion
  8.4 1.1 copy.25
  9.5 0.1 copy.28
  9.6 1.1 copy.26
  10.8 0.1 copy.29
  10.9 0.0 copy-done.1
  10.9 0.2 copy.27
  11.1 0.1 copy.30
  11.3 0.5 fusion.4
  11.7 1.0 copy.31
  12.8 0.0 copy-start
  12.8 2.6 reshape.88
  15.4 5.2 %all-to-all-start = ((bf16[8,48,1536]{2,1,0:T(8,128)(2,1)}), bf16[8,48,1536]{2,1,0:T(8,128)(2,1)S(1)}, u32[]{:S(2)}, u32[]{:S(2)}) async-start(bf16[8,48,1536]{2,1,0:T(8,128)(2,1)} %reshape.88), calls=%async_computation | async-start | bytes 2359296 | tf_op jit(solution)/shard_map/all_to_all | solution.py:73
  20.6 0.0 copy-done
  20.6 1.7 convolution_convert_fusion.2
  22.3 15.1 %all-to-all-done = bf16[8,48,1536]{2,1,0:T(8,128)(2,1)S(1)} async-done(((bf16[8,48,1536]{2,1,0:T(8,128)(2,1)}), bf16[8,48,1536]{2,1,0:T(8,128)(2,1)S(1)}, u32[]{:S(2)}, u32[]{:S(2)}) %all-to-all-start) | async-done | bytes 1179680 | tf_op jit(solution)/shard_map/all_to_all | solution.py:73
  37.4 4.3 %all-to-all-start.2 = ((bf16[8,48,2048]{2,1,0:T(8,128)(2,1)}), bf16[8,48,2048]{2,1,0:T(8,128)(2,1)}, u32[]{:S(2)}, u32[]{:S(2)}) async-start(bf16[8,48,2048]{2,1,0:T(8,128)(2,1)} %bitcast.19), calls=%async_computation.2 | async-start | bytes 3145728 | tf_op jit(solution)/shard_map/all_to_all | solution.py:72
  41.7 0.0 reduce-scatter.2.cloned.1.call-start
  41.8 0.9 reshape.89
  42.6 1.7 fusion.30
  44.4 0.4 fusion.8
  44.8 0.1 maximum_bitcast_fusion.2
  44.9 0.4 collective-permute-start
  45.2 2.0 collective-permute-done
  47.2 0.3 fusion.3
  47.5 0.9 copy.35
  48.4 14.4 %all-to-all-done.2 = bf16[8,48,2048]{2,1,0:T(8,128)(2,1)} async-done(((bf16[8,48,2048]{2,1,0:T(8,128)(2,1)}), bf16[8,48,2048]{2,1,0:T(8,128)(2,1)}, u32[]{:S(2)}, u32[]{:S(2)}) %all-to-all-start.2) | async-done | bytes 1572896 | tf_op jit(solution)/shard_map/all_to_all | solution.py:72
  62.8 8.3 %convolution_convert_fusion = bf16[2048,2048]{1,0:T(8,128)(2,1)} fusion(bf16[384,2048]{1,0:T(8,128)(2,1)} %bitcast.20, bf16[384,2048]{0,1:T(8,128)(2,1)S(1)} %bitcast.54), kind=kOutput, calls=%fused_computation | convolution fusion | flops 3225419776 | bytes 11534336 | tf_op jit(solution)/shard_map/dot_general | solution.py:101
  71.1 0.0 reduce-scatter.2.cloned.1.call-update
  71.1 0.2 all-gather.2.cloned.1.call-start
  71.3 143.8 %reduce-scatter.2.cloned.1.call-done = bf16[512,2048]{1,0:T(8,128)(2,1)} async-done(((bf16[2048,2048]{1,0:T(8,128)(2,1)}), bf16[512,2048]{1,0:T(8,128)(2,1)}) %reduce-scatter.2.cloned.1.call-update) | async-done | bytes 2097168 | tf_op jit(solution)/shard_map/reduce_scatter | solution.py:100
  215.1 12.4 %multiply_subtract_fusion = (f32[512,2048]{1,0:T(8,128)}, f32[512,2048]{1,0:T(8,128)}, f32[512,2048]{1,0:T(8,128)}, bf16[512,2048]{1,0:T(8,128)(2,1)}) fusion(f32[512,2048]{1,0:T(8,128)} %param.15, bf16[512,2048]{1,0:T(8,128)(2,1)} %reduce-scatter.2.cloned.1.call-done, f32[512,2048]{1,0:T(8,128)} %param.17, f32[512,2048]{1,0:T(8,128)} %param.16), kind=kLoop, calls=%fused_computation.7 | loop fusion | flops 14680064 | bytes 29360128 | tf_op jit(solution)/shard_map/sub | solution.py:113
  227.5 0.0 all-gather.2.cloned.1.call-update
  227.5 150.5 %all-gather.2.cloned.1.call-done = bf16[2048,2048]{1,0:T(8,128)(2,1)} async-done(((bf16[512,2048]{1,0:T(8,128)(2,1)}), bf16[2048,2048]{1,0:T(8,128)(2,1)}) %all-gather.2.cloned.1.call-update) | async-done | bytes 8388624 | tf_op jit(solution)/shard_map/all_gather | solution.py:91
  378.1 6.8 %convolution_convert_fusion.1 = bf16[384,2048]{1,0:T(8,128)(2,1)S(1)} fusion(bf16[384,2048]{0,1:T(8,128)(2,1)S(1)} %bitcast.55, bf16[2048,2048]{1,0:T(8,128)(2,1)} %all-gather.2.cloned.1.call-done), kind=kOutput, calls=%fused_computation.8 | convolution fusion | flops 3222011904 | bytes 11534336 | tf_op jit(solution)/shard_map/dot_general | solution.py:89
  384.9 24.4 %all_to_all.15 = bf16[8,48,2048]{2,1,0:T(8,128)(2,1)S(1)} all-to-all(bf16[8,48,2048]{2,1,0:T(8,128)(2,1)S(1)} %bitcast.56), channel_id=1, replica_groups=mesh['rep'=4,'exp'=8] {'exp'}, dimensions={0} | all-to-all | bytes 3145728 | tf_op jit(solution)/shard_map/all_to_all | solution.py:96
  409.3 1.6 copy.55
  411.0 1.2 dot_general.22
  412.2 1.5 fusion
  (2 shorter events, 0.0 us)
Async XLA Ops:
  7.2 3.8 copy-start.1
  12.8 7.8 %copy-start = (bf16[128,4096]{1,0:T(8,128)(2,1)S(1)}, bf16[128,4096]{1,0:T(8,128)(2,1)}, u32[]{:S(2)}) copy-start(bf16[128,4096]{1,0:T(8,128)(2,1)} %param.9) | copy-start | bytes 3145732
  15.4 22.0 %all-to-all-start = ((bf16[8,48,1536]{2,1,0:T(8,128)(2,1)}), bf16[8,48,1536]{2,1,0:T(8,128)(2,1)S(1)}, u32[]{:S(2)}, u32[]{:S(2)}) async-start(bf16[8,48,1536]{2,1,0:T(8,128)(2,1)} %reshape.88), calls=%async_computation | async-start | bytes 2359296 | tf_op jit(solution)/shard_map/all_to_all | solution.py:73
  37.4 25.4 %all-to-all-start.2 = ((bf16[8,48,2048]{2,1,0:T(8,128)(2,1)}), bf16[8,48,2048]{2,1,0:T(8,128)(2,1)}, u32[]{:S(2)}, u32[]{:S(2)}) async-start(bf16[8,48,2048]{2,1,0:T(8,128)(2,1)} %bitcast.19), calls=%async_computation.2 | async-start | bytes 3145728 | tf_op jit(solution)/shard_map/all_to_all | solution.py:72
  41.7 173.4 %reduce-scatter.2.cloned.1.call-start = ((), (), s32[]{:S(2)}) async-start(), calls=%async_computation.5 | async-start | bytes 10485760 | tf_op jit(solution)/shard_map/reduce_scatter | solution.py:100
  44.9 2.4 collective-permute-start
  71.1 307.0 %all-gather.2.cloned.1.call-start = ((), (), s32[]{:S(2)}) async-start(), calls=%async_computation.4 | async-start | bytes 10485760 | tf_op jit(solution)/shard_map/all_gather | solution.py:91
Sparse Core Ops, SparseCore 0:
  71.2 143.8 reduce-scatter.1
  227.7 150.3 all-gather.1
where the time goes:
time: 421 us
  waiting for transfers between devices  326 us (77%)
  blocking collectives  24.4 us (6%)
  matrix products  18.8 us (4%)
  other arithmetic  14.3 us (3%)
  between operations  14.2 us (3%)
  local copies, waits for them, and re-layouts  12.8 us (3%)
  starting transfers between devices  10.1 us (2%)
    all_gather x1, waiting for transfers between devices, body(): lax.all_gather(shard_bf, 'rep', axis=0, tiled=True)  151 us
    reduce_scatter x1, waiting for transfers between devices, body(): lax.psum_scatter(lax.dot_general(x_rows, grads_flat, (((0,), (0,)), ((),...  144 us
    all_to_all x1, blocking collectives, body(): lax.all_to_all(dx_send, 'exp', split_axis=0, concat_axis=0, tiled=True)  24.4 us
    all_to_all x1, waiting for transfers between devices, body(): lax.all_to_all(parts, 'exp', split_axis=0, concat_axis=0, tiled=True)  15.1 us
    all_to_all x1, waiting for transfers between devices, body(): lax.all_to_all(x_send, 'exp', split_axis=0, concat_axis=0, tiled=True)  14.4 us
    sub x1, other arithmetic, body(): new_master = master - learn_rate * update  12.4 us
  transfers between devices with their start and end apart: 5, of which 5 were waited for; matrix products, arithmetic and copies ran while one was open for 1% of the time, Pallas kernels for 0%

commit v1 on v0

--- a/solution.py
+++ b/solution.py
@@ -1,6 +1,8 @@
 import jax
 import jax.numpy as jnp
 from jax import lax
+from jax.experimental import pallas as pl
+from jax.experimental.pallas import tpu as pltpu
 from jax.sharding import PartitionSpec as P
 
 EXPERTS = 4
@@ -34,7 +36,7 @@
     return jnp.stack([grad_gate, grad_up], axis=1)
 
 
-def body(
+def weights_move(
     activations,
     grad_hidden,
     pre_gate,
@@ -114,6 +116,340 @@
     return (input_grad, new_master, new_first, new_second)
 
 
+MESH = pl.DeviceIdType.MESH
+VMEM_GRANT = 56 * 2**20
+
+
+def flip(position, mask, count):
+    out = 0
+    bit = 1
+    while bit < count:
+        have = position // bit % 2
+        out = out + bit * ((1 - have) if mask & bit else have)
+        bit *= 2
+    return out
+
+
+def rows_kernel(
+    x_ref, g_ref, r_ref, master_ref,
+    dx_ref, wg_ref,
+    gz, xz, rz, ps, rb, ph, wf, wb, xt, db, bk, us, fin,
+    g_send, g_recv, x_send, x_recv, r_send, r_recv,
+    p_send, p_recv, h_send, h_recv, b_send, b_recv, u_send, u_recv, w_sem,
+):
+    n = lax.axis_size("rep")
+    q = lax.axis_size("exp")
+    z = lax.axis_index("rep")
+    me = lax.axis_index("exp")
+    group = q // EXPERTS
+    e_me = me // group
+    c_me = me % group
+    tok = x_ref.shape[0]
+    width = x_ref.shape[1]
+    piece = master_ref.shape[0]
+    hid2 = master_ref.shape[1]
+    half = hid2 // group
+    strip = width // group
+    slots = EXPERTS * CAP
+    rows = q * CAP
+    layers = [flip(z, k, n) for k in range(n)]
+
+    weights = pltpu.make_async_copy(master_ref, wf, w_sem)
+    weights.start()
+
+    barrier = pltpu.get_barrier_semaphore()
+    for k in range(1, n):
+        pl.semaphore_signal(barrier, inc=1, device_id={"rep": layers[k]}, device_id_type=MESH)
+    for j in range(1, q):
+        pl.semaphore_signal(barrier, inc=1, device_id={"exp": (me + j) % q}, device_id_type=MESH)
+    gz[z] = g_ref[...]
+    pl.semaphore_wait(barrier, n + q - 2)
+
+    def columns(c, layer):
+        return pl.ds(pl.multiple_of(c * strip + layer * piece, piece), piece)
+
+    def g_copy(way, step):
+        block = z - step if way == 0 else z + step
+        to = z + 1 if way == 0 else z - 1
+        return pltpu.make_async_remote_copy(
+            src_ref=gz.at[block], dst_ref=gz.at[block],
+            send_sem=g_send.at[way, step], recv_sem=g_recv.at[way, step],
+            device_id={"rep": to}, device_id_type=MESH,
+        )
+
+    def g_sends(way, step):
+        return (z >= step) & (z < n - 1) if way == 0 else (z + step < n) & (z > 0)
+
+    def g_lands(way, step):
+        return z - 1 - step >= 0 if way == 0 else z + 1 + step < n
+
+    def r_copy(k):
+        return pltpu.make_async_remote_copy(
+            src_ref=rz.at[0], dst_ref=rz.at[k], send_sem=r_send.at[k], recv_sem=r_recv.at[k],
+            device_id={"rep": layers[k]}, device_id_type=MESH,
+        )
+
+    def x_copy(k, c):
+        return pltpu.make_async_remote_copy(
+            src_ref=x_ref.at[:, columns(c, layers[k])], dst_ref=xz.at[k, c],
+            send_sem=x_send.at[k, c], recv_sem=x_recv.at[k, c],
+            device_id={"rep": layers[k]}, device_id_type=MESH,
+        )
+
+    def p_copy(k, j):
+        to = (me + j) % q
+        return pltpu.make_async_remote_copy(
+            src_ref=ps.at[k, to // group, to % group], dst_ref=rb.at[k, me],
+            send_sem=p_send.at[k, j], recv_sem=p_recv.at[k, j],
+            device_id={"exp": to}, device_id_type=MESH,
+        )
+
+    def h_copy(k, m):
+        to = e_me * group + (c_me + group - m) % group
+        return pltpu.make_async_remote_copy(
+            src_ref=rb.at[k, :, :, pl.ds(0, half)], dst_ref=ph.at[m - 1, k],
+            send_sem=h_send.at[k, m], recv_sem=h_recv.at[k, m],
+            device_id={"exp": to}, device_id_type=MESH,
+        )
+
+    def b_copy(k, j):
+        to = (me + j) % q
+        return pltpu.make_async_remote_copy(
+            src_ref=db.at[k, to], dst_ref=bk.at[k, c_me, e_me],
+            send_sem=b_send.at[k, j], recv_sem=b_recv.at[k, j],
+            device_id={"exp": to}, device_id_type=MESH,
+        )
+
+    def u_copy(k):
+        return pltpu.make_async_remote_copy(
+            src_ref=us.at[k], dst_ref=fin.at[k], send_sem=u_send.at[k], recv_sem=u_recv.at[k],
+            device_id={"rep": layers[k]}, device_id_type=MESH,
+        )
+
+    def g_start(step):
+        for way in range(2):
+            @pl.when(g_sends(way, step))
+            def _():
+                g_copy(way, step).start()
+
+    def g_land(step):
+        for way in range(2):
+            @pl.when(g_lands(way, step))
+            def _():
+                g_copy(way, step).wait_recv()
+
+    def pack(k):
+        if k:
+            r_copy(k).wait_recv()
+            for c in range(group):
+                x_copy(k, c).wait_recv()
+        route = rz[k]
+        for c in range(group):
+            part = jnp.dot(
+                route, gz[layers[k], :, c * half : (c + 1) * half],
+                preferred_element_type=jnp.float32,
+            )
+            ps[k, :, c, :, :half] = part.astype(jnp.bfloat16).reshape(EXPERTS, CAP, half)
+            part = jnp.dot(route, xz[k, c], preferred_element_type=jnp.float32)
+            ps[k, :, c, :, half:] = part.astype(jnp.bfloat16).reshape(EXPERTS, CAP, piece)
+        for j in range(1, q):
+            p_copy(k, j).start()
+        rb[k, me] = ps[k, e_me, c_me]
+
+    def exchange(k):
+        for j in range(1, q):
+            p_copy(k, j).wait_recv()
+        for m in range(1, group):
+            h_copy(k, m).start()
+        xt[:, k * rows : (k + 1) * rows] = rb[k, :, :, half:].reshape(rows, piece).T
+
+    def grads_of(k, m):
+        if m == 0:
+            return rb[k, :, :, :half].reshape(rows, half)
+        return ph[m - 1, k].reshape(rows, half)
+
+    def hidden_at(m):
+        return pl.ds(pl.multiple_of((c_me + m) % group * half, half), half)
+
+    def input_rows(k):
+        total = None
+        for m in range(group):
+            if m:
+                h_copy(k, m).wait_recv()
+            part = lax.dot_general(
+                grads_of(k, m), wb[:, hidden_at(m)], (((1,), (1,)), ((), ())),
+                preferred_element_type=jnp.float32,
+            )
+            total = part if total is None else total + part
+        db[k] = total.astype(jnp.bfloat16).reshape(q, CAP, piece)
+        for j in range(1, q):
+            b_copy(k, j).start()
+        bk[k, c_me, e_me] = db[k, me]
+
+    def unpack(k):
+        for j in range(1, q):
+            b_copy(k, j).wait_recv()
+        for c in range(group):
+            part = lax.dot_general(
+                rz[k], bk[k, c].reshape(slots, piece), (((0,), (0,)), ((), ())),
+                preferred_element_type=jnp.float32,
+            )
+            part = part.astype(jnp.bfloat16)
+            if k:
+                us[k, c] = part
+            else:
+                dx_ref[:, columns(c, z)] = part
+        if k:
+            u_copy(k).start()
+
+    rz[0] = r_ref[...]
+    for k in range(1, n):
+        r_copy(k).start()
+    g_start(0)
+    for k in range(1, n):
+        for c in range(group):
+            x_copy(k, c).start()
+    for c in range(group):
+        xz[0, c] = x_ref[:, columns(c, z)]
+    pack(0)
+    weights.wait()
+    wb[...] = wf[...].astype(jnp.bfloat16)
+    for k in range(1, n + 4):
+        if k < n:
+            g_land(k - 1)
+            if k < n - 1:
+                g_start(k)
+            pack(k)
+        if 0 <= k - 1 < n:
+            exchange(k - 1)
+        if 0 <= k - 2 < n:
+            input_rows(k - 2)
+        if k == n + 1:
+            for m in range(group):
+                for k2 in range(0, half, 256):
+                    acc = None
+                    for b in range(n):
+                        lhs = xt[:, b * rows : (b + 1) * rows]
+                        if m == 0:
+                            rhs = rb[b, :, :, k2 : k2 + 256]
+                        else:
+                            rhs = ph[m - 1, b, :, :, k2 : k2 + 256]
+                        part = jnp.dot(lhs, rhs.reshape(rows, 256), preferred_element_type=jnp.float32)
+                        acc = part if acc is None else acc + part
+                    at = pl.multiple_of((c_me + m) % group * half + k2, 256)
+                    wg_ref[:, pl.ds(at, 256)] = acc
+        if 0 <= k - 4 < n:
+            unpack(k - 4)
+    for k in range(1, n):
+        u_copy(k).wait_recv()
+        for c in range(group):
+            dx_ref[:, columns(c, layers[k])] = fin[k, c]
+
+    for step in range(n - 1):
+        for way in range(2):
+            @pl.when(g_sends(way, step))
+            def _():
+                g_copy(way, step).wait_send()
+    for k in range(n):
+        if k:
+            r_copy(k).wait_send()
+            for c in range(group):
+                x_copy(k, c).wait_send()
+            u_copy(k).wait_send()
+        for j in range(1, q):
+            p_copy(k, j).wait_send()
+            b_copy(k, j).wait_send()
+        for m in range(1, group):
+            h_copy(k, m).wait_send()
+
+
+def tokens_move(
+    activations,
+    grad_hidden,
+    pre_gate,
+    pre_up,
+    modality,
+    expert_index,
+    master,
+    first_moment,
+    second_moment,
+):
+    n = lax.axis_size("rep")
+    q = lax.axis_size("exp")
+    group = q // EXPERTS
+    tok, width = activations.shape
+    piece, hid2 = master.shape
+    half = hid2 // group
+    expert = 2 * modality + expert_index
+    onehot = (expert[:, None] == jnp.arange(EXPERTS, dtype=jnp.int32)[None, :]).astype(jnp.int32)
+    before = jnp.cumsum(onehot, axis=0) - onehot
+    slot_pos = jnp.sum(before * onehot, axis=1)
+    place = expert * CAP + slot_pos
+    routing = place[None, :] == jnp.arange(EXPERTS * CAP, dtype=jnp.int32)[:, None]
+    routing = routing.astype(jnp.bfloat16)
+    grads = hidden_grads(jnp.stack([grad_hidden, pre_gate, pre_up], axis=1)).reshape(tok, hid2)
+    vmem = pl.BlockSpec(memory_space=pltpu.VMEM)
+    bf16 = jnp.bfloat16
+    dma = pltpu.SemaphoreType.DMA
+    input_grad, weight_grad = pl.pallas_call(
+        rows_kernel,
+        out_shape=(
+            jax.ShapeDtypeStruct((tok, width), bf16),
+            jax.ShapeDtypeStruct((piece, hid2), jnp.float32),
+        ),
+        in_specs=[vmem, vmem, vmem, pl.BlockSpec(memory_space=pl.ANY)],
+        out_specs=(vmem, vmem),
+        scratch_shapes=[
+            pltpu.VMEM((n, tok, hid2), bf16),
+            pltpu.VMEM((n, group, tok, piece), bf16),
+            pltpu.VMEM((n, EXPERTS * CAP, tok), bf16),
+            pltpu.VMEM((n, EXPERTS, group, CAP, half + piece), bf16),
+            pltpu.VMEM((n, q, CAP, half + piece), bf16),
+            pltpu.VMEM((group - 1, n, q, CAP, half), bf16),
+            pltpu.VMEM((piece, hid2), jnp.float32),
+            pltpu.VMEM((piece, hid2), bf16),
+            pltpu.VMEM((piece, n * q * CAP), bf16),
+            pltpu.VMEM((n, q, CAP, piece), bf16),
+            pltpu.VMEM((n, group, EXPERTS, CAP, piece), bf16),
+            pltpu.VMEM((n, group, tok, piece), bf16),
+            pltpu.VMEM((n, group, tok, piece), bf16),
+            dma((2, n)), dma((2, n)),
+            dma((n, group)), dma((n, group)),
+            dma((n,)), dma((n,)),
+            dma((n, q)), dma((n, q)),
+            dma((n, group)), dma((n, group)),
+            dma((n, q)), dma((n, q)),
+            dma((n,)), dma((n,)),
+            dma,
+        ],
+        compiler_params=pltpu.CompilerParams(
+            collective_id=0, has_side_effects=True, vmem_limit_bytes=VMEM_GRANT
+        ),
+        name="rows_kernel",
+    )(activations, grads, routing, master)
+    new_first = beta_one * first_moment + (1.0 - beta_one) * weight_grad
+    new_second = beta_two * second_moment + (1.0 - beta_two) * weight_grad * weight_grad
+    corr_one = 1.0 - beta_one**adam_count
+    corr_two = 1.0 - beta_two**adam_count
+    update = new_first / corr_one / (jnp.sqrt(new_second / corr_two) + adam_eps)
+    new_master = master - learn_rate * update
+    return (input_grad, new_master, new_first, new_second)
+
+
+def body(*blocks):
+    n = lax.axis_size("rep")
+    q = lax.axis_size("exp")
+    group = q // EXPERTS
+    tok, width = blocks[0].shape
+    piece, hid2 = blocks[6].shape
+    held = n * q * CAP * (hid2 + 4 * piece) * 2 + 12 * piece * hid2
+    held += n * tok * (hid2 + 3 * group * piece) * 2 + n * EXPERTS * CAP * group * hid2
+    fits = held <= VMEM_GRANT * 3 // 4 and group >= 2 and n & (n - 1) == 0
+    if fits and piece % 128 == 0 and hid2 // group % 256 == 0 and q * CAP % 128 == 0:
+        return tokens_move(*blocks)
+    return weights_move(*blocks)
+
+
 def solution(mesh):
     in_specs = (
         P(("rep", "exp"), None),

time: 421 us -> 140 us (0.33)
  the two profiles are of different devices: /device:TPU:0 before, /device:TPU:13 now
where the time goes in v1:
time: 140 us
  Pallas kernels  125 us (89%)
  other arithmetic  12 us (9%)
  local copies, waits for them, and re-layouts  1.82 us (1%)
    pallas_call x1, Pallas kernels, tokens_move(): pl.pallas_call(rows_kernel, out_shape=(jax.ShapeDtypeStruct((tok, width),...  125 us
    sub x1, other arithmetic, tokens_move(): new_master = master - learn_rate * update  8.78 us

profile of v1, /device:TPU:13, one launch (start us, length us, event | category | flops | bytes accessed | tf_op | source)
XLA Modules:
  0.0 139.5 jit_solution(8238416452591371629)
XLA Ops:
  0.6 0.7 multiply_add_fusion.2
  1.3 0.1 fusion.13
  1.4 0.2 reduce_window_sum.11
  1.6 0.2 select_reduce_fusion
  1.8 0.6 fusion.12.r_ref
  2.4 1.4 fusion.11
  3.8 0.0 copy-start
  3.8 0.1 maximum_bitcast_fusion
  3.9 0.8 copy.14
  4.7 125.0 %rows_kernel.1 = (bf16[128,4096]{1,0:T(8,128)(2,1)}, f32[512,2048]{1,0:T(8,128)}) custom-call(bf16[128,4096]{1,0:T(8,128)(2,1)} %x_ref.1, bf16[128,2048]{1,0:T(8,128)(2,1)} %bitcast.7, bf16[192,128]{1,0:T(8,128)(2,1)} %fusion.12.r_ref, f32[512,2048]{1,0:T(8,128)} %master_ref.1), custom_call_target="tpu_custom_call" | custom-call | tf_op jit(solution)/shard_map/rows_kernel/pallas_call | solution.py:394
  129.7 0.0 copy-done
  129.8 0.0 copy-start.1
  129.8 8.8 %multiply_subtract_fusion = (f32[512,2048]{1,0:T(8,128)}, f32[512,2048]{1,0:T(8,128)}, f32[512,2048]{1,0:T(8,128)}) fusion(f32[512,2048]{1,0:T(8,128)S(1)} %copy-done, f32[512,2048]{1,0:T(8,128)} %get-tuple-element.7, f32[512,2048]{1,0:T(8,128)} %param.17, f32[512,2048]{1,0:T(8,128)} %param.16), kind=kLoop, calls=%fused_computation.2 | loop fusion | flops 12582912 | bytes 29360128 | tf_op jit(solution)/shard_map/sub | solution.py:435
  138.5 0.0 copy-done.1
  138.5 1.0 copy.16
  (1 shorter events, 0.0 us)
Async XLA Ops:
  3.8 125.9 %copy-start = (f32[512,2048]{1,0:T(8,128)S(1)}, f32[512,2048]{1,0:T(8,128)}, u32[]{:S(2)}) copy-start(f32[512,2048]{1,0:T(8,128)} %master_ref.1) | copy-start | bytes 12582916
  129.8 8.8 %copy-start.1 = (bf16[128,4096]{1,0:T(8,128)(2,1)S(1)}, bf16[128,4096]{1,0:T(8,128)(2,1)}, u32[]{:S(2)}) copy-start(bf16[128,4096]{1,0:T(8,128)(2,1)} %get-tuple-element.17) | copy-start | bytes 3145732

commit v2 on v1

--- a/solution.py
+++ b/solution.py
@@ -131,11 +131,12 @@
 
 
 def rows_kernel(
-    x_ref, g_ref, r_ref, master_ref,
+    x_ref, grad_ref, gate_ref, up_ref, r_ref, master_ref,
     dx_ref, wg_ref,
-    gz, xz, rz, ps, rb, ph, wf, wb, xt, db, bk, us, fin,
+    gz, xz, rz, ps, rb, qs, xb, ph, wf, wb, xt, acc_ref, db, bk, us, fin,
     g_send, g_recv, x_send, x_recv, r_send, r_recv,
-    p_send, p_recv, h_send, h_recv, b_send, b_recv, u_send, u_recv, w_sem,
+    p_send, p_recv, q_send, q_recv, h_send, h_recv,
+    b_send, b_recv, u_send, u_recv, own_sem, tile_sem, w_sem,
 ):
     n = lax.axis_size("rep")
     q = lax.axis_size("exp")
@@ -154,6 +155,12 @@
     rows = q * CAP
     layers = [flip(z, k, n) for k in range(n)]
 
+    def columns(c, layer):
+        return pl.ds(pl.multiple_of(c * strip + layer * piece, piece), piece)
+
+    def own_copy(c):
+        return pltpu.make_async_copy(x_ref.at[:, columns(c, z)], xz.at[0, c], own_sem.at[c])
+
     weights = pltpu.make_async_copy(master_ref, wf, w_sem)
     weights.start()
 
@@ -162,11 +169,20 @@
         pl.semaphore_signal(barrier, inc=1, device_id={"rep": layers[k]}, device_id_type=MESH)
     for j in range(1, q):
         pl.semaphore_signal(barrier, inc=1, device_id={"exp": (me + j) % q}, device_id_type=MESH)
-    gz[z] = g_ref[...]
+    for c in range(group):
+        own_copy(c).start()
+    hidden = grad_ref.shape[1]
+    for at in range(0, hidden, 256):
+        grad_val = grad_ref[:, at : at + 256].astype(jnp.float32)
+        gate_val = gate_ref[:, at : at + 256].astype(jnp.float32)
+        up_val = up_ref[:, at : at + 256].astype(jnp.float32)
+        sig = 1.0 / (1.0 + jnp.exp(-gate_val))
+        grad_gate = grad_val * up_val * sig * (1.0 + gate_val * (1.0 - sig))
+        gz[z, :, at : at + 256] = grad_gate.astype(jnp.bfloat16)
+        grad_up = grad_val * gate_val * sig
+        gz[z, :, hidden + at : hidden + at + 256] = grad_up.astype(jnp.bfloat16)
+    rz[0] = r_ref[...]
     pl.semaphore_wait(barrier, n + q - 2)
-
-    def columns(c, layer):
-        return pl.ds(pl.multiple_of(c * strip + layer * piece, piece), piece)
 
     def g_copy(way, step):
         block = z - step if way == 0 else z + step
@@ -204,10 +220,18 @@
             device_id={"exp": to}, device_id_type=MESH,
         )
 
+    def q_copy(k, j):
+        to = (me + j) % q
+        return pltpu.make_async_remote_copy(
+            src_ref=qs.at[k, to // group, to % group], dst_ref=xb.at[k, me],
+            send_sem=q_send.at[k, j], recv_sem=q_recv.at[k, j],
+            device_id={"exp": to}, device_id_type=MESH,
+        )
+
     def h_copy(k, m):
         to = e_me * group + (c_me + group - m) % group
         return pltpu.make_async_remote_copy(
-            src_ref=rb.at[k, :, :, pl.ds(0, half)], dst_ref=ph.at[m - 1, k],
+            src_ref=rb.at[k], dst_ref=ph.at[m - 1, k],
             send_sem=h_send.at[k, m], recv_sem=h_recv.at[k, m],
             device_id={"exp": to}, device_id_type=MESH,
         )
@@ -241,31 +265,72 @@
     def pack(k):
         if k:
             r_copy(k).wait_recv()
-            for c in range(group):
-                x_copy(k, c).wait_recv()
         route = rz[k]
         for c in range(group):
             part = jnp.dot(
                 route, gz[layers[k], :, c * half : (c + 1) * half],
                 preferred_element_type=jnp.float32,
             )
-            ps[k, :, c, :, :half] = part.astype(jnp.bfloat16).reshape(EXPERTS, CAP, half)
-            part = jnp.dot(route, xz[k, c], preferred_element_type=jnp.float32)
-            ps[k, :, c, :, half:] = part.astype(jnp.bfloat16).reshape(EXPERTS, CAP, piece)
+            ps[k, :, c] = part.astype(jnp.bfloat16).reshape(EXPERTS, CAP, half)
         for j in range(1, q):
             p_copy(k, j).start()
         rb[k, me] = ps[k, e_me, c_me]
+
+    def x_starts(k):
+        for c in range(group):
+            x_copy(k, c).start()
+
+    def x_pack(k):
+        for c in range(group):
+            if k:
+                x_copy(k, c).wait_recv()
+            else:
+                own_copy(c).wait()
+            part = jnp.dot(rz[k], xz[k, c], preferred_element_type=jnp.float32)
+            qs[k, :, c] = part.astype(jnp.bfloat16).reshape(EXPERTS, CAP, piece)
+        for j in range(1, q):
+            q_copy(k, j).start()
+        xb[k, me] = qs[k, e_me, c_me]
+
+    def x_turn(k):
+        for j in range(1, q):
+            q_copy(k, j).wait_recv()
+        xt[:, k * rows : (k + 1) * rows] = xb[k].reshape(rows, piece).T
 
     def exchange(k):
         for j in range(1, q):
             p_copy(k, j).wait_recv()
         for m in range(1, group):
             h_copy(k, m).start()
-        xt[:, k * rows : (k + 1) * rows] = rb[k, :, :, half:].reshape(rows, piece).T
+
+    def tile_copy(m, at):
+        start = pl.multiple_of((c_me + m) % group * half + at, 256)
+        return pltpu.make_async_copy(
+            acc_ref.at[:, m * half + at : m * half + at + 256], wg_ref.at[:, pl.ds(start, 256)],
+            tile_sem.at[(m * half + at) // 256],
+        )
+
+    def weight_rows(first, last):
+        for m in range(group):
+            for at in range(0, half, 256):
+                total = None
+                for k in range(first, last):
+                    lhs = xt[:, k * rows : (k + 1) * rows]
+                    if m == 0:
+                        rhs = rb[k, :, :, at : at + 256]
+                    else:
+                        rhs = ph[m - 1, k, :, :, at : at + 256]
+                    part = jnp.dot(lhs, rhs.reshape(rows, 256), preferred_element_type=jnp.float32)
+                    total = part if total is None else total + part
+                if first:
+                    total = total + acc_ref[:, m * half + at : m * half + at + 256]
+                acc_ref[:, m * half + at : m * half + at + 256] = total
+                if last == n:
+                    tile_copy(m, at).start()
 
     def grads_of(k, m):
         if m == 0:
-            return rb[k, :, :, :half].reshape(rows, half)
+            return rb[k].reshape(rows, half)
         return ph[m - 1, k].reshape(rows, half)
 
     def hidden_at(m):
@@ -302,48 +367,48 @@
         if k:
             u_copy(k).start()
 
-    rz[0] = r_ref[...]
+    g_start(0)
     for k in range(1, n):
         r_copy(k).start()
-    g_start(0)
-    for k in range(1, n):
-        for c in range(group):
-            x_copy(k, c).start()
-    for c in range(group):
-        xz[0, c] = x_ref[:, columns(c, z)]
     pack(0)
+    x_pack(0)
     weights.wait()
     wb[...] = wf[...].astype(jnp.bfloat16)
-    for k in range(1, n + 4):
-        if k < n:
-            g_land(k - 1)
-            if k < n - 1:
-                g_start(k)
-            pack(k)
-        if 0 <= k - 1 < n:
-            exchange(k - 1)
-        if 0 <= k - 2 < n:
+    for k in range(1, n):
+        g_land(k - 1)
+        if k < n - 1:
+            g_start(k)
+        pack(k)
+        if k == n - 1:
+            for later in range(max(n - 2, 1), n):
+                x_starts(later)
+        elif k >= 2:
+            x_starts(k - 1)
+        exchange(k - 1)
+        if k >= 2:
             input_rows(k - 2)
-        if k == n + 1:
-            for m in range(group):
-                for k2 in range(0, half, 256):
-                    acc = None
-                    for b in range(n):
-                        lhs = xt[:, b * rows : (b + 1) * rows]
-                        if m == 0:
-                            rhs = rb[b, :, :, k2 : k2 + 256]
-                        else:
-                            rhs = ph[m - 1, b, :, :, k2 : k2 + 256]
-                        part = jnp.dot(lhs, rhs.reshape(rows, 256), preferred_element_type=jnp.float32)
-                        acc = part if acc is None else acc + part
-                    at = pl.multiple_of((c_me + m) % group * half + k2, 256)
-                    wg_ref[:, pl.ds(at, 256)] = acc
-        if 0 <= k - 4 < n:
-            unpack(k - 4)
+    exchange(n - 1)
+    input_rows(n - 2)
+    input_rows(n - 1)
+    for k in range(n - 1):
+        unpack(k)
+        if k + 1 < n - 1:
+            x_pack(k + 1)
+    unpack(n - 1)
+    x_pack(n - 1)
+    for k in range(n // 2):
+        x_turn(k)
+    weight_rows(0, n // 2)
+    for k in range(n // 2, n):
+        x_turn(k)
+    weight_rows(n // 2, n)
     for k in range(1, n):
         u_copy(k).wait_recv()
         for c in range(group):
             dx_ref[:, columns(c, layers[k])] = fin[k, c]
+    for m in range(group):
+        for at in range(0, half, 256):
+            tile_copy(m, at).wait()
 
     for step in range(n - 1):
         for way in range(2):
@@ -358,6 +423,7 @@
             u_copy(k).wait_send()
         for j in range(1, q):
             p_copy(k, j).wait_send()
+            q_copy(k, j).wait_send()
             b_copy(k, j).wait_send()
         for m in range(1, group):
             h_copy(k, m).wait_send()
@@ -387,8 +453,8 @@
     place = expert * CAP + slot_pos
     routing = place[None, :] == jnp.arange(EXPERTS * CAP, dtype=jnp.int32)[:, None]
     routing = routing.astype(jnp.bfloat16)
-    grads = hidden_grads(jnp.stack([grad_hidden, pre_gate, pre_up], axis=1)).reshape(tok, hid2)
     vmem = pl.BlockSpec(memory_space=pltpu.VMEM)
+    anywhere = pl.BlockSpec(memory_space=pl.ANY)
     bf16 = jnp.bfloat16
     dma = pltpu.SemaphoreType.DMA
     input_grad, weight_grad = pl.pallas_call(
@@ -397,18 +463,21 @@
             jax.ShapeDtypeStruct((tok, width), bf16),
             jax.ShapeDtypeStruct((piece, hid2), jnp.float32),
         ),
-        in_specs=[vmem, vmem, vmem, pl.BlockSpec(memory_space=pl.ANY)],
-        out_specs=(vmem, vmem),
+        in_specs=[anywhere, vmem, vmem, vmem, vmem, anywhere],
+        out_specs=(vmem, anywhere),
         scratch_shapes=[
             pltpu.VMEM((n, tok, hid2), bf16),
             pltpu.VMEM((n, group, tok, piece), bf16),
             pltpu.VMEM((n, EXPERTS * CAP, tok), bf16),
-            pltpu.VMEM((n, EXPERTS, group, CAP, half + piece), bf16),
-            pltpu.VMEM((n, q, CAP, half + piece), bf16),
+            pltpu.VMEM((n, EXPERTS, group, CAP, half), bf16),
+            pltpu.VMEM((n, q, CAP, half), bf16),
+            pltpu.VMEM((n, EXPERTS, group, CAP, piece), bf16),
+            pltpu.VMEM((n, q, CAP, piece), bf16),
             pltpu.VMEM((group - 1, n, q, CAP, half), bf16),
             pltpu.VMEM((piece, hid2), jnp.float32),
             pltpu.VMEM((piece, hid2), bf16),
             pltpu.VMEM((piece, n * q * CAP), bf16),
+            pltpu.VMEM((piece, hid2), jnp.float32),
             pltpu.VMEM((n, q, CAP, piece), bf16),
             pltpu.VMEM((n, group, EXPERTS, CAP, piece), bf16),
             pltpu.VMEM((n, group, tok, piece), bf16),
@@ -417,16 +486,18 @@
             dma((n, group)), dma((n, group)),
             dma((n,)), dma((n,)),
             dma((n, q)), dma((n, q)),
+            dma((n, q)), dma((n, q)),
             dma((n, group)), dma((n, group)),
             dma((n, q)), dma((n, q)),
             dma((n,)), dma((n,)),
+            dma((group,)), dma((hid2 // 256,)),
             dma,
         ],
         compiler_params=pltpu.CompilerParams(
             collective_id=0, has_side_effects=True, vmem_limit_bytes=VMEM_GRANT
         ),
         name="rows_kernel",
-    )(activations, grads, routing, master)
+    )(activations, grad_hidden, pre_gate, pre_up, routing, master)
     new_first = beta_one * first_moment + (1.0 - beta_one) * weight_grad
     new_second = beta_two * second_moment + (1.0 - beta_two) * weight_grad * weight_grad
     corr_one = 1.0 - beta_one**adam_count
@@ -444,8 +515,8 @@
     piece, hid2 = blocks[6].shape
     held = n * q * CAP * (hid2 + 4 * piece) * 2 + 12 * piece * hid2
     held += n * tok * (hid2 + 3 * group * piece) * 2 + n * EXPERTS * CAP * group * hid2
-    fits = held <= VMEM_GRANT * 3 // 4 and group >= 2 and n & (n - 1) == 0
-    if fits and piece % 128 == 0 and hid2 // group % 256 == 0 and q * CAP % 128 == 0:
+    fits = held <= VMEM_GRANT * 3 // 4 and group >= 2 and n >= 2 and n & (n - 1) == 0
+    if fits and piece % 128 == 0 and hid2 % 512 == 0 and hid2 // group % 256 == 0 and q * CAP % 128 == 0:
         return tokens_move(*blocks)
     return weights_move(*blocks)
 

time: 140 us -> 108 us (0.77)
  the two profiles are of different devices: /device:TPU:13 before, /device:TPU:0 now
where the time goes in v2:
time: 108 us
  Pallas kernels  95.4 us (88%)
  other arithmetic  10.5 us (10%)
    pallas_call x1, Pallas kernels, tokens_move(): pl.pallas_call(rows_kernel, out_shape=(jax.ShapeDtypeStruct((tok, width),...  95.4 us
    sub x1, other arithmetic, tokens_move(): new_master = master - learn_rate * update  8.78 us

profile of v2, /device:TPU:0, one launch (start us, length us, event | category | flops | bytes accessed | tf_op | source)
XLA Modules:
  0.0 107.6 jit_solution(2341846976608626332)
XLA Ops:
  0.6 0.7 multiply_add_fusion.2
  1.3 0.1 fusion.2
  1.4 0.2 reduce_window_sum.11
  1.6 0.0 copy-start
  1.6 0.2 select_reduce_fusion
  1.8 0.6 fusion.1.r_ref
  2.4 95.4 %rows_kernel.1 = (bf16[128,4096]{1,0:T(8,128)(2,1)}, f32[512,2048]{1,0:T(8,128)}) custom-call(bf16[128,4096]{1,0:T(8,128)(2,1)} %x_ref.1, bf16[128,1024]{1,0:T(8,128)(2,1)} %grad_ref.1, bf16[128,1024]{1,0:T(8,128)(2,1)} %gate_ref.1, bf16[128,1024]{1,0:T(8,128)(2,1)} %up_ref.1, bf16[192,128]{1,0:T(8,128)(2,1)} %fusion.1.r_ref, f32[512,2048]{1,0:T(8,128)} %master_ref.1), custom_call_target="tpu_custom_call" | custom-call | tf_op jit(solution)/shard_map/rows_kernel/pallas_call | solution.py:460
  97.9 0.0 copy-done
  97.9 0.0 copy-start.1
  97.9 8.8 %multiply_subtract_fusion = (f32[512,2048]{1,0:T(8,128)}, f32[512,2048]{1,0:T(8,128)}, f32[512,2048]{1,0:T(8,128)}) fusion(f32[512,2048]{1,0:T(8,128)S(1)} %copy-done, f32[512,2048]{1,0:T(8,128)} %get-tuple-element.7, f32[512,2048]{1,0:T(8,128)} %param.17, f32[512,2048]{1,0:T(8,128)} %param.16), kind=kLoop, calls=%fused_computation.2 | loop fusion | flops 12582912 | bytes 29360128 | tf_op jit(solution)/shard_map/sub | solution.py:506
  106.7 0.0 copy-done.1
  106.7 1.0 copy.14
  (1 shorter events, 0.0 us)
Async XLA Ops:
  1.6 96.3 %copy-start = (f32[512,2048]{1,0:T(8,128)S(1)}, f32[512,2048]{1,0:T(8,128)}, u32[]{:S(2)}) copy-start(f32[512,2048]{1,0:T(8,128)} %master_ref.1) | copy-start | bytes 12582916
  97.9 8.8 %copy-start.1 = (bf16[128,4096]{1,0:T(8,128)(2,1)S(1)}, bf16[128,4096]{1,0:T(8,128)(2,1)}, u32[]{:S(2)}) copy-start(bf16[128,4096]{1,0:T(8,128)(2,1)} %get-tuple-element.15) | copy-start | bytes 3145732

commit v3 on v2

--- a/solution.py
+++ b/solution.py
@@ -117,7 +117,7 @@
 
 
 MESH = pl.DeviceIdType.MESH
-VMEM_GRANT = 56 * 2**20
+VMEM_GRANT = 38 * 2**20
 
 
 def flip(position, mask, count):
@@ -133,7 +133,7 @@
 def rows_kernel(
     x_ref, grad_ref, gate_ref, up_ref, r_ref, master_ref,
     dx_ref, wg_ref,
-    gz, xz, rz, ps, rb, qs, xb, ph, wf, wb, xt, acc_ref, db, bk, us, fin,
+    gz, xz, rz, ps, rb, qs, xb, ph, wf, wb, xt, db, bk, us, fin,
     g_send, g_recv, x_send, x_recv, r_send, r_recv,
     p_send, p_recv, q_send, q_recv, h_send, h_recv,
     b_send, b_recv, u_send, u_recv, own_sem, tile_sem, w_sem,
@@ -184,12 +184,15 @@
     rz[0] = r_ref[...]
     pl.semaphore_wait(barrier, n + q - 2)
 
-    def g_copy(way, step):
+    def hidden_at(m):
+        return pl.ds(pl.multiple_of((c_me + m) % group * half, half), half)
+
+    def g_copy(way, step, m):
         block = z - step if way == 0 else z + step
         to = z + 1 if way == 0 else z - 1
         return pltpu.make_async_remote_copy(
-            src_ref=gz.at[block], dst_ref=gz.at[block],
-            send_sem=g_send.at[way, step], recv_sem=g_recv.at[way, step],
+            src_ref=gz.at[block, :, hidden_at(m)], dst_ref=gz.at[block, :, hidden_at(m)],
+            send_sem=g_send.at[way, step, m], recv_sem=g_recv.at[way, step, m],
             device_id={"rep": to}, device_id_type=MESH,
         )
 
@@ -213,11 +216,12 @@
         )
 
     def p_copy(k, j):
-        to = (me + j) % q
-        return pltpu.make_async_remote_copy(
-            src_ref=ps.at[k, to // group, to % group], dst_ref=rb.at[k, me],
+        to_e = (e_me + j // group) % EXPERTS
+        to_c = (c_me + j % group) % group
+        return pltpu.make_async_remote_copy(
+            src_ref=ps.at[k, to_e, to_c], dst_ref=rb.at[k, me],
             send_sem=p_send.at[k, j], recv_sem=p_recv.at[k, j],
-            device_id={"exp": to}, device_id_type=MESH,
+            device_id={"exp": to_e * group + to_c}, device_id_type=MESH,
         )
 
     def q_copy(k, j):
@@ -250,35 +254,34 @@
             device_id={"rep": layers[k]}, device_id_type=MESH,
         )
 
-    def g_start(step):
+    def g_start(step, m):
         for way in range(2):
             @pl.when(g_sends(way, step))
             def _():
-                g_copy(way, step).start()
-
-    def g_land(step):
+                g_copy(way, step, m).start()
+
+    def g_land(step, m):
         for way in range(2):
             @pl.when(g_lands(way, step))
             def _():
-                g_copy(way, step).wait_recv()
-
-    def pack(k):
-        if k:
-            r_copy(k).wait_recv()
-        route = rz[k]
-        for c in range(group):
-            part = jnp.dot(
-                route, gz[layers[k], :, c * half : (c + 1) * half],
-                preferred_element_type=jnp.float32,
-            )
-            ps[k, :, c] = part.astype(jnp.bfloat16).reshape(EXPERTS, CAP, half)
-        for j in range(1, q):
-            p_copy(k, j).start()
-        rb[k, me] = ps[k, e_me, c_me]
-
-    def x_starts(k):
-        for c in range(group):
-            x_copy(k, c).start()
+                g_copy(way, step, m).wait_recv()
+
+    def pack(k, m):
+        part = jnp.dot(rz[k], gz[layers[k], :, hidden_at(m)], preferred_element_type=jnp.float32)
+        ps[k, :, (c_me + m) % group] = part.astype(jnp.bfloat16).reshape(EXPERTS, CAP, half)
+        for j in range(m, q, group):
+            if j:
+                p_copy(k, j).start()
+        if m == 0:
+            rb[k, me] = ps[k, e_me, c_me]
+
+    def x_starts(step):
+        for k in range(1, n):
+            to = layers[k]
+            @pl.when(((to > z) & (to == step)) | ((to < z) & (to == n - 1 - step)))
+            def _():
+                for c in range(group):
+                    x_copy(k, c).start()
 
     def x_pack(k):
         for c in range(group):
@@ -306,7 +309,7 @@
     def tile_copy(m, at):
         start = pl.multiple_of((c_me + m) % group * half + at, 256)
         return pltpu.make_async_copy(
-            acc_ref.at[:, m * half + at : m * half + at + 256], wg_ref.at[:, pl.ds(start, 256)],
+            wf.at[:, m * half + at : m * half + at + 256], wg_ref.at[:, pl.ds(start, 256)],
             tile_sem.at[(m * half + at) // 256],
         )
 
@@ -323,8 +326,8 @@
                     part = jnp.dot(lhs, rhs.reshape(rows, 256), preferred_element_type=jnp.float32)
                     total = part if total is None else total + part
                 if first:
-                    total = total + acc_ref[:, m * half + at : m * half + at + 256]
-                acc_ref[:, m * half + at : m * half + at + 256] = total
+                    total = total + wf[:, m * half + at : m * half + at + 256]
+                wf[:, m * half + at : m * half + at + 256] = total
                 if last == n:
                     tile_copy(m, at).start()
 
@@ -332,9 +335,6 @@
         if m == 0:
             return rb[k].reshape(rows, half)
         return ph[m - 1, k].reshape(rows, half)
-
-    def hidden_at(m):
-        return pl.ds(pl.multiple_of((c_me + m) % group * half, half), half)
 
     def input_rows(k):
         total = None
@@ -367,35 +367,40 @@
         if k:
             u_copy(k).start()
 
-    g_start(0)
+    for m in range(group):
+        g_start(0, m)
     for k in range(1, n):
         r_copy(k).start()
-    pack(0)
+    for m in range(group):
+        pack(0, m)
     x_pack(0)
     weights.wait()
     wb[...] = wf[...].astype(jnp.bfloat16)
     for k in range(1, n):
-        g_land(k - 1)
-        if k < n - 1:
-            g_start(k)
-        pack(k)
-        if k == n - 1:
-            for later in range(max(n - 2, 1), n):
-                x_starts(later)
-        elif k >= 2:
-            x_starts(k - 1)
+        r_copy(k).wait_recv()
+        for m in range(group):
+            g_land(k - 1, m)
+            if k < n - 1:
+                g_start(k, m)
+            pack(k, m)
+        x_starts(k)
         exchange(k - 1)
         if k >= 2:
             input_rows(k - 2)
+        if k >= 3:
+            unpack(k - 3)
+    input_rows(n - 2)
+    for k in range(max(n - 3, 0), n - 2):
+        unpack(k)
     exchange(n - 1)
-    input_rows(n - 2)
+    x_pack(1)
     input_rows(n - 1)
-    for k in range(n - 1):
-        unpack(k)
-        if k + 1 < n - 1:
-            x_pack(k + 1)
+    unpack(n - 2)
+    for k in range(2, n - 1):
+        x_pack(k)
     unpack(n - 1)
-    x_pack(n - 1)
+    if n > 2:
+        x_pack(n - 1)
     for k in range(n // 2):
         x_turn(k)
     weight_rows(0, n // 2)
@@ -414,7 +419,8 @@
         for way in range(2):
             @pl.when(g_sends(way, step))
             def _():
-                g_copy(way, step).wait_send()
+                for m in range(group):
+                    g_copy(way, step, m).wait_send()
     for k in range(n):
         if k:
             r_copy(k).wait_send()
@@ -477,12 +483,11 @@
             pltpu.VMEM((piece, hid2), jnp.float32),
             pltpu.VMEM((piece, hid2), bf16),
             pltpu.VMEM((piece, n * q * CAP), bf16),
-            pltpu.VMEM((piece, hid2), jnp.float32),
             pltpu.VMEM((n, q, CAP, piece), bf16),
             pltpu.VMEM((n, group, EXPERTS, CAP, piece), bf16),
             pltpu.VMEM((n, group, tok, piece), bf16),
             pltpu.VMEM((n, group, tok, piece), bf16),
-            dma((2, n)), dma((2, n)),
+            dma((2, n, group)), dma((2, n, group)),
             dma((n, group)), dma((n, group)),
             dma((n,)), dma((n,)),
             dma((n, q)), dma((n, q)),
@@ -515,7 +520,7 @@
     piece, hid2 = blocks[6].shape
     held = n * q * CAP * (hid2 + 4 * piece) * 2 + 12 * piece * hid2
     held += n * tok * (hid2 + 3 * group * piece) * 2 + n * EXPERTS * CAP * group * hid2
-    fits = held <= VMEM_GRANT * 3 // 4 and group >= 2 and n >= 2 and n & (n - 1) == 0
+    fits = held <= VMEM_GRANT and group >= 2 and n >= 2 and n & (n - 1) == 0
     if fits and piece % 128 == 0 and hid2 % 512 == 0 and hid2 // group % 256 == 0 and q * CAP % 128 == 0:
         return tokens_move(*blocks)
     return weights_move(*blocks)

time: 108 us -> 108 us (level)
  the two profiles are of different devices: /device:TPU:0 before, /device:TPU:25 now
where the time goes in v3:
time: 108 us; the launch traced here: 107 us
  Pallas kernels  91.3 us (85%)
  other arithmetic  8.24 us (8%)
  local copies, waits for them, and re-layouts  7.23 us (7%)
    pallas_call x1, Pallas kernels, tokens_move(): pl.pallas_call(rows_kernel, out_shape=(jax.ShapeDtypeStruct((tok, width),...  91.3 us
    unnamed x13, local copies, waits for them, and re-layouts  7.23 us
    sub x1, other arithmetic, tokens_move(): new_master = master - learn_rate * update  7.11 us

profile of v3, /device:TPU:25, one launch (start us, length us, event | category | flops | bytes accessed | tf_op | source)
XLA Modules:
  0.0 107.4 jit_solution(5313958221205681520)
XLA Ops:
  0.6 0.7 multiply_add_fusion.2
  1.3 0.1 fusion.2
  1.4 0.2 reduce_window_sum.11
  1.6 0.2 select_reduce_fusion
  1.8 0.0 copy-start
  1.8 2.2 %copy-done = f32[512,2048]{1,0:T(8,128)S(1)} copy-done((f32[512,2048]{1,0:T(8,128)S(1)}, f32[512,2048]{1,0:T(8,128)}, u32[]{:S(2)}) %copy-start) | copy-done | bytes 4194328
  4.0 0.0 copy-start.1
  4.0 1.2 %copy-done.1 = bf16[128,4096]{1,0:T(8,128)(2,1)S(1)} copy-done((bf16[128,4096]{1,0:T(8,128)(2,1)S(1)}, bf16[128,4096]{1,0:T(8,128)(2,1)}, u32[]{:S(2)}) %copy-start.1) | copy-done | bytes 1048600
  5.2 0.0 copy-start.2
  5.2 0.9 copy-done.2
  6.2 0.0 copy-start.3
  6.2 0.9 copy-done.3
  7.1 0.0 copy-start.4
  7.1 0.9 copy-done.4
  8.1 0.0 copy-start.5
  8.1 91.3 %rows_kernel.1 = (bf16[128,4096]{1,0:T(8,128)(2,1)S(1)}, f32[512,2048]{1,0:T(8,128)S(1)}) custom-call(bf16[128,4096]{1,0:T(8,128)(2,1)S(1)} %copy-done.1, bf16[128,1024]{1,0:T(8,128)(2,1)S(1)} %copy-done.2, bf16[128,1024]{1,0:T(8,128)(2,1)S(1)} %copy-done.3, bf16[128,1024]{1,0:T(8,128)(2,1)S(1)} %copy-done.4, bf16[192,128]{1,0:T(8,128)(2,1)S(1)} %fusion.1.r_ref, ...), custom_call_target="tpu_custom_call" | custom-call | tf_op jit(solution)/shard_map/rows_kernel/pallas_call | solution.py:466
  99.3 0.0 copy-done.5
  99.3 7.1 %multiply_subtract_fusion = (f32[512,2048]{1,0:T(8,128)}, f32[512,2048]{1,0:T(8,128)}, f32[512,2048]{1,0:T(8,128)}) fusion(f32[512,2048]{1,0:T(8,128)S(1)} %copy-done, f32[512,2048]{1,0:T(8,128)S(1)} %get-tuple-element.7, f32[512,2048]{1,0:T(8,128)S(1)} %copy-done.5, f32[512,2048]{1,0:T(8,128)} %param.16), kind=kLoop, calls=%fused_computation.2 | loop fusion | flops 12582912 | bytes 29360128 | tf_op jit(solution)/shard_map/sub | solution.py:511
  106.4 1.0 copy.14
  (2 shorter events, 0.0 us)
Async XLA Ops:
  1.8 2.2 %copy-start = (f32[512,2048]{1,0:T(8,128)S(1)}, f32[512,2048]{1,0:T(8,128)}, u32[]{:S(2)}) copy-start(f32[512,2048]{1,0:T(8,128)} %master_ref.1) | copy-start | bytes 12582916
  4.0 1.2 %copy-start.1 = (bf16[128,4096]{1,0:T(8,128)(2,1)S(1)}, bf16[128,4096]{1,0:T(8,128)(2,1)}, u32[]{:S(2)}) copy-start(bf16[128,4096]{1,0:T(8,128)(2,1)} %x_ref.1) | copy-start | bytes 3145732
  5.2 0.9 copy-start.2
  6.2 0.9 copy-start.3
  7.1 0.9 copy-start.4
  8.1 91.3 %copy-start.5 = (f32[512,2048]{1,0:T(8,128)S(1)}, f32[512,2048]{1,0:T(8,128)}, u32[]{:S(2)}) copy-start(f32[512,2048]{1,0:T(8,128)} %param.17) | copy-start | bytes 12582916

commit v4 on v3

--- a/solution.py
+++ b/solution.py
@@ -117,7 +117,7 @@
 
 
 MESH = pl.DeviceIdType.MESH
-VMEM_GRANT = 38 * 2**20
+VMEM_GRANT = 56 * 2**20
 
 
 def flip(position, mask, count):
@@ -131,7 +131,7 @@
 
 
 def rows_kernel(
-    x_ref, grad_ref, gate_ref, up_ref, r_ref, master_ref,
+    x_ref, grad_ref, gate_ref, up_ref, mode_ref, index_ref, master_ref,
     dx_ref, wg_ref,
     gz, xz, rz, ps, rb, qs, xb, ph, wf, wb, xt, db, bk, us, fin,
     g_send, g_recv, x_send, x_recv, r_send, r_recv,
@@ -181,7 +181,18 @@
         gz[z, :, at : at + 256] = grad_gate.astype(jnp.bfloat16)
         grad_up = grad_val * gate_val * sig
         gz[z, :, hidden + at : hidden + at + 256] = grad_up.astype(jnp.bfloat16)
-    rz[0] = r_ref[...]
+    expert = 2 * mode_ref[...] + index_ref[...]
+    lanes = lax.broadcasted_iota(jnp.int32, (tok, tok), 1)
+    earlier = lax.broadcasted_iota(jnp.int32, (tok, tok), 0) < lanes
+    onehot = lax.broadcasted_iota(jnp.int32, (16, tok), 0) == expert
+    onehot = onehot.astype(jnp.float32)
+    before = jnp.dot(
+        onehot.astype(jnp.bfloat16), earlier.astype(jnp.float32).astype(jnp.bfloat16),
+        preferred_element_type=jnp.float32,
+    )
+    place = expert.astype(jnp.float32) * CAP + jnp.sum(before * onehot, axis=0, keepdims=True)
+    slot = lax.broadcasted_iota(jnp.int32, (slots, tok), 0).astype(jnp.float32)
+    rz[0] = (slot == place).astype(jnp.float32).astype(jnp.bfloat16)
     pl.semaphore_wait(barrier, n + q - 2)
 
     def hidden_at(m):
@@ -275,10 +286,13 @@
         if m == 0:
             rb[k, me] = ps[k, e_me, c_me]
 
-    def x_starts(step):
+    at_end = (z == 0) | (z == n - 1)
+
+    def x_starts(step, who=None):
         for k in range(1, n):
             to = layers[k]
-            @pl.when(((to > z) & (to == step)) | ((to < z) & (to == n - 1 - step)))
+            free = ((to > z) & (to == step)) | ((to < z) & (to == n - 1 - step))
+            @pl.when(free if who is None else free & who)
             def _():
                 for c in range(group):
                     x_copy(k, c).start()
@@ -383,7 +397,7 @@
             if k < n - 1:
                 g_start(k, m)
             pack(k, m)
-        x_starts(k)
+        x_starts(k, at_end if k == n - 1 else None)
         exchange(k - 1)
         if k >= 2:
             input_rows(k - 2)
@@ -393,6 +407,7 @@
     for k in range(max(n - 3, 0), n - 2):
         unpack(k)
     exchange(n - 1)
+    x_starts(n - 1, jnp.logical_not(at_end))
     x_pack(1)
     input_rows(n - 1)
     unpack(n - 2)
@@ -452,13 +467,6 @@
     tok, width = activations.shape
     piece, hid2 = master.shape
     half = hid2 // group
-    expert = 2 * modality + expert_index
-    onehot = (expert[:, None] == jnp.arange(EXPERTS, dtype=jnp.int32)[None, :]).astype(jnp.int32)
-    before = jnp.cumsum(onehot, axis=0) - onehot
-    slot_pos = jnp.sum(before * onehot, axis=1)
-    place = expert * CAP + slot_pos
-    routing = place[None, :] == jnp.arange(EXPERTS * CAP, dtype=jnp.int32)[:, None]
-    routing = routing.astype(jnp.bfloat16)
     vmem = pl.BlockSpec(memory_space=pltpu.VMEM)
     anywhere = pl.BlockSpec(memory_space=pl.ANY)
     bf16 = jnp.bfloat16
@@ -469,7 +477,7 @@
             jax.ShapeDtypeStruct((tok, width), bf16),
             jax.ShapeDtypeStruct((piece, hid2), jnp.float32),
         ),
-        in_specs=[anywhere, vmem, vmem, vmem, vmem, anywhere],
+        in_specs=[anywhere, vmem, vmem, vmem, vmem, vmem, anywhere],
         out_specs=(vmem, anywhere),
         scratch_shapes=[
             pltpu.VMEM((n, tok, hid2), bf16),
@@ -502,7 +510,10 @@
             collective_id=0, has_side_effects=True, vmem_limit_bytes=VMEM_GRANT
         ),
         name="rows_kernel",
-    )(activations, grad_hidden, pre_gate, pre_up, routing, master)
+    )(
+        activations, grad_hidden, pre_gate, pre_up,
+        modality.reshape(1, tok), expert_index.reshape(1, tok), master,
+    )
     new_first = beta_one * first_moment + (1.0 - beta_one) * weight_grad
     new_second = beta_two * second_moment + (1.0 - beta_two) * weight_grad * weight_grad
     corr_one = 1.0 - beta_one**adam_count
@@ -520,7 +531,7 @@
     piece, hid2 = blocks[6].shape
     held = n * q * CAP * (hid2 + 4 * piece) * 2 + 12 * piece * hid2
     held += n * tok * (hid2 + 3 * group * piece) * 2 + n * EXPERTS * CAP * group * hid2
-    fits = held <= VMEM_GRANT and group >= 2 and n >= 2 and n & (n - 1) == 0
+    fits = held <= VMEM_GRANT * 3 // 4 and group >= 2 and n >= 2 and n & (n - 1) == 0
     if fits and piece % 128 == 0 and hid2 % 512 == 0 and hid2 // group % 256 == 0 and q * CAP % 128 == 0:
         return tokens_move(*blocks)
     return weights_move(*blocks)

time: 108 us -> 120 us (1.11)
  the two profiles are of different devices: /device:TPU:25 before, /device:TPU:0 now
where the time goes in v4:
time: 120 us; the launch traced here: 119 us
  Pallas kernels  109 us (91%)
  other arithmetic  8.78 us (7%)
    pallas_call x1, Pallas kernels, tokens_move(): pl.pallas_call(rows_kernel, out_shape=(jax.ShapeDtypeStruct((tok, width),...  109 us
    sub x1, other arithmetic, tokens_move(): new_master = master - learn_rate * update  8.78 us

profile of v4, /device:TPU:0, one launch (start us, length us, event | category | flops | bytes accessed | tf_op | source)
XLA Modules:
  0.0 119.1 jit_solution(2931905339261235523)
XLA Ops:
  0.6 0.0 copy-start
  0.6 108.7 %rows_kernel.1 = (bf16[128,4096]{1,0:T(8,128)(2,1)}, f32[512,2048]{1,0:T(8,128)}) custom-call(bf16[128,4096]{1,0:T(8,128)(2,1)} %x_ref.1, bf16[128,1024]{1,0:T(8,128)(2,1)} %grad_ref.1, bf16[128,1024]{1,0:T(8,128)(2,1)} %gate_ref.1, bf16[128,1024]{1,0:T(8,128)(2,1)} %up_ref.1, s32[1,128]{1,0:T(1,128)} %bitcast.2, s32[1,128]{1,0:T(1,128)} %bitcast.3, ...), custom_call_target="tpu_custom_call" | custom-call | tf_op jit(solution)/shard_map/rows_kernel/pallas_call | solution.py:474
  109.3 0.0 copy-done
  109.3 0.0 copy-start.1
  109.3 8.8 %multiply_subtract_fusion = (f32[512,2048]{1,0:T(8,128)}, f32[512,2048]{1,0:T(8,128)}, f32[512,2048]{1,0:T(8,128)}) fusion(f32[512,2048]{1,0:T(8,128)S(1)} %copy-done, f32[512,2048]{1,0:T(8,128)} %get-tuple-element.7, f32[512,2048]{1,0:T(8,128)} %param.17, f32[512,2048]{1,0:T(8,128)} %param.16), kind=kLoop, calls=%fused_computation.2 | loop fusion | flops 12582912 | bytes 29360128 | tf_op jit(solution)/shard_map/sub | solution.py:522
  118.1 0.0 copy-done.1
  118.1 1.0 copy.14
Async XLA Ops:
  0.6 108.7 %copy-start = (f32[512,2048]{1,0:T(8,128)S(1)}, f32[512,2048]{1,0:T(8,128)}, u32[]{:S(2)}) copy-start(f32[512,2048]{1,0:T(8,128)} %master_ref.1) | copy-start | bytes 12582916
  109.3 8.8 %copy-start.1 = (bf16[128,4096]{1,0:T(8,128)(2,1)S(1)}, bf16[128,4096]{1,0:T(8,128)(2,1)}, u32[]{:S(2)}) copy-start(bf16[128,4096]{1,0:T(8,128)(2,1)} %get-tuple-element.15) | copy-start | bytes 3145732

commit v5 on v4

--- a/solution.py
+++ b/solution.py
@@ -286,13 +286,10 @@
         if m == 0:
             rb[k, me] = ps[k, e_me, c_me]
 
-    at_end = (z == 0) | (z == n - 1)
-
-    def x_starts(step, who=None):
+    def x_starts(step):
         for k in range(1, n):
             to = layers[k]
-            free = ((to > z) & (to == step)) | ((to < z) & (to == n - 1 - step))
-            @pl.when(free if who is None else free & who)
+            @pl.when(((to > z) & (to == step)) | ((to < z) & (to == n - 1 - step)))
             def _():
                 for c in range(group):
                     x_copy(k, c).start()
@@ -397,7 +394,7 @@
             if k < n - 1:
                 g_start(k, m)
             pack(k, m)
-        x_starts(k, at_end if k == n - 1 else None)
+        x_starts(k)
         exchange(k - 1)
         if k >= 2:
             input_rows(k - 2)
@@ -407,7 +404,6 @@
     for k in range(max(n - 3, 0), n - 2):
         unpack(k)
     exchange(n - 1)
-    x_starts(n - 1, jnp.logical_not(at_end))
     x_pack(1)
     input_rows(n - 1)
     unpack(n - 2)

time: 120 us -> 102 us (0.85)
  Pallas kernels: 109 us -> 89.6 us
    pallas_call x1, Pallas kernels: 109 us -> 89.6 us  [tokens_move(): pl.pallas_call(rows_kernel, out_shape=(jax.ShapeDtypeStruct((tok, width),...]
where the time goes in v5:
time: 102 us; the launch traced here: 100 us
  Pallas kernels  89.6 us (88%)
  other arithmetic  8.78 us (9%)
    pallas_call x1, Pallas kernels, tokens_move(): pl.pallas_call(rows_kernel, out_shape=(jax.ShapeDtypeStruct((tok, width),...  89.6 us
    sub x1, other arithmetic, tokens_move(): new_master = master - learn_rate * update  8.78 us

profile of v5, /device:TPU:0, one launch (start us, length us, event | category | flops | bytes accessed | tf_op | source)
XLA Modules:
  0.0 100.0 jit_solution(14074087004946083412)
XLA Ops:
  0.6 0.0 copy-start
  0.6 89.6 %rows_kernel.1 = (bf16[128,4096]{1,0:T(8,128)(2,1)}, f32[512,2048]{1,0:T(8,128)}) custom-call(bf16[128,4096]{1,0:T(8,128)(2,1)} %x_ref.1, bf16[128,1024]{1,0:T(8,128)(2,1)} %grad_ref.1, bf16[128,1024]{1,0:T(8,128)(2,1)} %gate_ref.1, bf16[128,1024]{1,0:T(8,128)(2,1)} %up_ref.1, s32[1,128]{1,0:T(1,128)} %bitcast.2, s32[1,128]{1,0:T(1,128)} %bitcast.3, ...), custom_call_target="tpu_custom_call" | custom-call | tf_op jit(solution)/shard_map/rows_kernel/pallas_call | solution.py:470
  90.2 0.0 copy-done
  90.2 0.0 copy-start.1
  90.3 8.8 %multiply_subtract_fusion = (f32[512,2048]{1,0:T(8,128)}, f32[512,2048]{1,0:T(8,128)}, f32[512,2048]{1,0:T(8,128)}) fusion(f32[512,2048]{1,0:T(8,128)S(1)} %copy-done, f32[512,2048]{1,0:T(8,128)} %get-tuple-element.7, f32[512,2048]{1,0:T(8,128)} %param.17, f32[512,2048]{1,0:T(8,128)} %param.16), kind=kLoop, calls=%fused_computation.2 | loop fusion | flops 12582912 | bytes 29360128 | tf_op jit(solution)/shard_map/sub | solution.py:518
  99.0 0.0 copy-done.1
  99.0 1.0 copy.14
Async XLA Ops:
  0.6 89.6 %copy-start = (f32[512,2048]{1,0:T(8,128)S(1)}, f32[512,2048]{1,0:T(8,128)}, u32[]{:S(2)}) copy-start(f32[512,2048]{1,0:T(8,128)} %master_ref.1) | copy-start | bytes 12582916
  90.2 8.8 %copy-start.1 = (bf16[128,4096]{1,0:T(8,128)(2,1)S(1)}, bf16[128,4096]{1,0:T(8,128)(2,1)}, u32[]{:S(2)}) copy-start(bf16[128,4096]{1,0:T(8,128)(2,1)} %get-tuple-element.15) | copy-start | bytes 3145732
